TPU v7x, 32 devices: a whole 2x2x4 slice. The times are simulated.
32 devices in a mesh: ctx: 2 (over core), head: 4 (over y, x), exp: 4 (over z).
Axes of the slice: x: 2, y: 2, z: 4, core: 2. Of those that a mesh axis runs over, the one named last changes fastest.
Arguments:
- query_heads: bfloat16 [4, 4, 256, 4, 512], P('exp', None, 'ctx', 'head'), may hold values from -180 to 180
- key_heads: bfloat16 [4, 4, 256, 4, 128], P('exp', None, 'ctx', 'head'), may hold values from -6 to 6
- value_heads: bfloat16 [4, 4, 256, 4, 128], P('exp', None, 'ctx', 'head'), may hold values from -6 to 6
- hidden_state: bfloat16 [4, 4, 256, 2048], P('exp', 'head', 'ctx'), may hold values from -6 to 6
- output_grad: bfloat16 [4, 4, 256, 2048], P('exp', 'head', 'ctx'), may hold values from -6 to 6
- norm_gain: float32 [2048], replicated, may hold values from 0.5 to 1.5
- expert_ids: int32 [4, 4, 256, 8], P('exp', 'head', 'ctx'), may hold values from 0 to 31, all different within a row; in each aligned block of 128 rows (0 to 127, 128 to 255, ..., all dimensions but the last counted through in order) at most 36 rows name the same one
- gate_probs: float32 [4, 4, 256, 8], P('exp', 'head', 'ctx'), may hold values from 0.02 to 0.4
- out_weight: bfloat16 [4, 512, 2048], P('head'), may hold values from -0.125 to 0.125
- gate_weight: bfloat16 [32, 2048, 768], P(('ctx', 'head', 'exp')), may hold values from -0.125 to 0.125
- up_weight: bfloat16 [32, 2048, 768], P(('ctx', 'head', 'exp')), may hold values from -0.125 to 0.125
- down_weight: bfloat16 [32, 768, 2048], P(('ctx', 'head', 'exp')), may hold values from -0.21875 to 0.21875
Outputs:
- query_gradient: bfloat16 [4, 4, 256, 4, 512], P('exp', None, 'ctx', 'head')
- key_gradient: bfloat16 [4, 4, 256, 4, 128], P('exp', None, 'ctx', 'head')
- value_gradient: bfloat16 [4, 4, 256, 4, 128], P('exp', None, 'ctx', 'head')
- hidden_grad: bfloat16 [4, 4, 256, 2048], P('exp', 'head', 'ctx')
- gain_grad: float32 [2048], replicated
- proj_grad: bfloat16 [4, 512, 2048], P('head', ('ctx', 'exp'))
- gate_grad: bfloat16 [32, 2048, 768], P(('ctx', 'head', 'exp'))
- up_grad: bfloat16 [32, 2048, 768], P(('ctx', 'head', 'exp'))
- down_grad: bfloat16 [32, 768, 2048], P(('ctx', 'head', 'exp'))
Inputs may be any that keep to these rules, and one draw needn't show every extreme that they name: `expert_ids`: each token names 8 different experts; the 128 tokens of one sequence on one index of ctx name one expert at most 36 times, and some such group names some expert exactly 36 times.
All inputs are finite; a program needn't handle non-finite values.
Results may differ from a plain program's by a relative error of at most 0.034.
Values may be sent and summed in bfloat16 or wider, within the bound.
A program may use at most 192 MiB of HBM per device.

v0:
```python
import jax
import jax.numpy as jnp
from jax import lax
from jax.sharding import PartitionSpec as P

NORM_EPS = 1e-06
FLOOR_SCORE = -1e30
ROWS_DIMS = (((0,), (0,)), ((), ()))
LAST_DIMS = (((1,), (1,)), ((), ()))


def slot_capacity(token_rows, choices, experts):
    mean_load = (token_rows * choices + experts - 1) // experts
    return max(2, mean_load + max(1, mean_load // 8))


def heads_to_rows(block_vals, per_key, head_size):
    seq_count, block_len = (block_vals.shape[0], block_vals.shape[1])
    split_vals = block_vals.reshape(seq_count, block_len, per_key, head_size)
    return split_vals.transpose(0, 2, 1, 3).reshape(seq_count, per_key * block_len, head_size)


def rows_to_heads(row_vals, per_key, block_len):
    seq_count, head_size = (row_vals.shape[0], row_vals.shape[2])
    split_vals = row_vals.reshape(seq_count, per_key, block_len, head_size)
    return split_vals.transpose(0, 2, 1, 3).reshape(seq_count, block_len, per_key * head_size)


def expert_backward(rows_in, gate_mat, up_mat, down_mat, model_width):
    inputs = rows_in[:, :model_width]
    upstream = rows_in[:, model_width:]
    gate_val = jnp.dot(inputs, gate_mat, preferred_element_type=jnp.float32)
    up_val = jnp.dot(inputs, up_mat, preferred_element_type=jnp.float32)
    grad_act = lax.dot_general(upstream, down_mat, LAST_DIMS, preferred_element_type=jnp.float32)
    sigma_gate = jax.nn.sigmoid(gate_val)
    act_rows = (gate_val * sigma_gate * up_val).astype(jnp.bfloat16)
    up_part = (grad_act * gate_val * sigma_gate).astype(jnp.bfloat16)
    gate_part = (grad_act * up_val * sigma_gate * (1.0 + gate_val * (1.0 - sigma_gate))).astype(
        jnp.bfloat16
    )
    down_sum = lax.dot_general(act_rows, upstream, ROWS_DIMS, preferred_element_type=jnp.float32)
    gate_sum = lax.dot_general(inputs, gate_part, ROWS_DIMS, preferred_element_type=jnp.float32)
    up_sum = lax.dot_general(inputs, up_part, ROWS_DIMS, preferred_element_type=jnp.float32)
    back_rows = lax.dot_general(
        gate_part, gate_mat, LAST_DIMS, preferred_element_type=jnp.float32
    ) + lax.dot_general(up_part, up_mat, LAST_DIMS, preferred_element_type=jnp.float32)
    return (back_rows.astype(jnp.bfloat16), gate_sum, up_sum, down_sum)


def on_device(
    query_heads,
    key_heads,
    value_heads,
    hidden_state,
    output_grad,
    norm_gain,
    expert_ids,
    gate_probs,
    out_weight,
    gate_weight,
    up_weight,
    down_weight,
):
    model_width = hidden_state.shape[-1]
    token_rows = hidden_state.shape[2]
    choices = expert_ids.shape[-1]
    device_count = lax.axis_size(("ctx", "head", "exp"))
    capacity = slot_capacity(token_rows, choices, device_count)
    hidden_wide = hidden_state.reshape(token_rows, model_width).astype(jnp.float32)
    out_rows = output_grad.reshape(token_rows, model_width)
    inv_rms = lax.rsqrt(jnp.mean(hidden_wide * hidden_wide, axis=1, keepdims=True) + NORM_EPS)
    unit_rows = hidden_wide * inv_rms
    normed = (unit_rows * norm_gain).astype(jnp.bfloat16)
    probs_flat = gate_probs.reshape(token_rows, choices)
    expert_grad = (probs_flat[:, :, None] * out_rows.astype(jnp.float32)[:, None, :]).astype(
        jnp.bfloat16
    )
    flat_ids = expert_ids.reshape(-1)
    pick_count = flat_ids.shape[0]
    chosen = (flat_ids[:, None] == jnp.arange(device_count, dtype=jnp.int32)[None, :]).astype(
        jnp.bfloat16
    )
    earlier = (jnp.arange(pick_count)[:, None] > jnp.arange(pick_count)[None, :]).astype(
        jnp.bfloat16
    )
    before = jnp.dot(earlier, chosen, preferred_element_type=jnp.float32)
    slot_pos = jnp.sum(before * chosen.astype(jnp.float32), axis=1).astype(jnp.int32)
    target = flat_ids * capacity + slot_pos
    payload = jnp.concatenate(
        [jnp.repeat(normed, choices, axis=0), expert_grad.reshape(pick_count, model_width)], axis=1
    )
    outbox = (
        jnp.zeros((device_count * capacity, 2 * model_width), jnp.bfloat16).at[target].set(payload)
    )
    arrived = lax.all_to_all(
        outbox.reshape(device_count, capacity, 2 * model_width),
        ("ctx", "head", "exp"),
        split_axis=0,
        concat_axis=0,
        tiled=True,
    )
    back_rows, gate_sum, up_sum, down_sum = expert_backward(
        arrived.reshape(-1, 2 * model_width),
        gate_weight[0],
        up_weight[0],
        down_weight[0],
        model_width,
    )
    returned = lax.all_to_all(
        back_rows.reshape(device_count, capacity, model_width),
        ("ctx", "head", "exp"),
        split_axis=0,
        concat_axis=0,
        tiled=True,
    )
    picked_back = returned.reshape(device_count * capacity, model_width)[target]
    normed_grad = jnp.sum(
        picked_back.reshape(token_rows, choices, model_width).astype(jnp.float32), axis=1
    )
    gain_grad = lax.psum(jnp.sum(normed_grad * unit_rows, axis=0), ("ctx", "head", "exp"))
    scaled = normed_grad * norm_gain
    mixed_term = jnp.mean(scaled * unit_rows, axis=1, keepdims=True)
    hidden_rows = (
        out_rows.astype(jnp.float32) + inv_rms * (scaled - unit_rows * mixed_term)
    ).astype(jnp.bfloat16)
    hidden_grad = hidden_rows.reshape(hidden_state.shape)
    ctx_count = lax.axis_size("ctx")
    ctx_index = lax.axis_index("ctx")
    query_block = query_heads[0, :, :, 0, :]
    seq_count, block_len = (query_block.shape[0], query_block.shape[1])
    head_size = key_heads.shape[-1]
    per_key = query_block.shape[2] // head_size
    query_rows = heads_to_rows(query_block, per_key, head_size)
    row_count = query_rows.shape[1]
    score_scaling = head_size ** (-0.5)
    query_pos = ctx_index * block_len + jnp.tile(jnp.arange(block_len, dtype=jnp.int32), per_key)
    query_last = ctx_index * block_len + block_len - 1
    seq_len = block_len * ctx_count

    def piece_scores(key_piece):
        key_pos = jnp.arange(key_piece.shape[1], dtype=jnp.int32)
        allowed = key_pos[None, None, :] <= query_pos[None, :, None]
        attention_scores = (
            jnp.einsum("sqd,skd->sqk", query_rows, key_piece, preferred_element_type=jnp.float32)
            * score_scaling
        )
        return (attention_scores, allowed)

    initial = (
        jnp.full((seq_count, row_count), FLOOR_SCORE, jnp.float32),
        jnp.zeros((seq_count, row_count), jnp.float32),
        jnp.zeros((seq_count, row_count, head_size), jnp.float32),
    )
    pieces = (
        lax.all_gather(key_heads, "ctx", axis=2, tiled=True),
        lax.all_gather(value_heads, "ctx", axis=2, tiled=True),
    )
    key_piece = pieces[0][0, :, :, 0, :]
    value_piece = pieces[1][0, :, :, 0, :]

    def forward_update(current):
        run_max, run_sum, run_acc = current
        attention_scores, allowed = piece_scores(key_piece)
        new_max = jnp.maximum(
            run_max, jnp.max(jnp.where(allowed, attention_scores, FLOOR_SCORE), axis=2)
        )
        weight_matrices = jnp.where(allowed, jnp.exp(attention_scores - new_max[:, :, None]), 0.0)
        new_sum = jnp.sum(weight_matrices, axis=2)
        new_acc = jnp.einsum(
            "sqk,skd->sqd",
            weight_matrices,
            value_piece.astype(jnp.float32),
            precision=lax.Precision.HIGHEST,
        )
        return (new_max, new_sum, new_acc)

    run_max, run_sum, run_acc = lax.cond(
        jnp.int32(0) <= query_last, forward_update, lambda current: current, initial
    )
    log_sum = run_max + jnp.log(run_sum)
    attn_rows = (run_acc / run_sum[:, :, None]).astype(jnp.bfloat16)
    grad_block = lax.all_gather(hidden_grad, "head", axis=1, tiled=True)[0]
    grad_tokens = grad_block.reshape(seq_count * block_len, model_width)
    proj_mat = out_weight[0]
    attn_grad_tok = lax.dot_general(
        grad_tokens, proj_mat, LAST_DIMS, preferred_element_type=jnp.float32
    ).astype(jnp.bfloat16)
    attention_gradient = heads_to_rows(
        attn_grad_tok.reshape(seq_count, block_len, per_key * head_size), per_key, head_size
    )
    delta_rows = jnp.sum(
        attention_gradient.astype(jnp.float32) * attn_rows.astype(jnp.float32), axis=2
    )
    attn_tokens = rows_to_heads(attn_rows, per_key, block_len).reshape(
        seq_count * block_len, per_key * head_size
    )
    initial_grads = (
        jnp.zeros((seq_count, row_count, head_size), jnp.float32),
        jnp.zeros((seq_count, seq_len, head_size), jnp.float32),
        jnp.zeros((seq_count, seq_len, head_size), jnp.float32),
    )
    pieces = (
        lax.all_gather(key_heads, "ctx", axis=2, tiled=True),
        lax.all_gather(value_heads, "ctx", axis=2, tiled=True),
    )
    backward_key_piece = pieces[0][0, :, :, 0, :]
    backward_value_piece = pieces[1][0, :, :, 0, :]

    def backward_update(current):
        attention_scores, allowed = piece_scores(backward_key_piece)
        probability_values = jnp.where(
            allowed, jnp.exp(attention_scores - log_sum[:, :, None]), 0.0
        )
        value_part = jnp.einsum(
            "sqk,sqd->skd",
            probability_values.astype(jnp.bfloat16),
            attention_gradient,
            preferred_element_type=jnp.float32,
        )
        probability_gradient = jnp.einsum(
            "sqd,skd->sqk",
            attention_gradient,
            backward_value_piece,
            preferred_element_type=jnp.float32,
        )
        score_gradient = (
            probability_values * (probability_gradient - delta_rows[:, :, None])
        ).astype(jnp.bfloat16)
        query_acc = (
            jnp.einsum(
                "sqk,skd->sqd",
                score_gradient,
                backward_key_piece,
                preferred_element_type=jnp.float32,
            )
            * score_scaling
        )
        key_part = (
            jnp.einsum(
                "sqk,sqd->skd", score_gradient, query_rows, preferred_element_type=jnp.float32
            )
            * score_scaling
        )
        return (query_acc, key_part, value_part)

    query_acc, key_acc, value_acc = lax.cond(
        jnp.int32(0) <= query_last, backward_update, lambda current: current, initial_grads
    )
    proj_full = lax.dot_general(
        attn_tokens, grad_tokens, ROWS_DIMS, preferred_element_type=jnp.float32
    )
    key_total, value_total, proj_mid = (
        lax.psum_scatter(
            key_acc.astype(jnp.bfloat16), "ctx", scatter_dimension=1, tiled=True
        ).astype(jnp.float32),
        lax.psum_scatter(
            value_acc.astype(jnp.bfloat16), "ctx", scatter_dimension=1, tiled=True
        ).astype(jnp.float32),
        lax.psum_scatter(
            proj_full.astype(jnp.bfloat16), "ctx", scatter_dimension=0, tiled=True
        ).astype(jnp.float32),
    )
    proj_part = lax.psum_scatter(
        proj_mid.astype(jnp.bfloat16), "exp", scatter_dimension=0, tiled=True
    )
    query_gradient = (
        rows_to_heads(query_acc, per_key, block_len).astype(jnp.bfloat16).reshape(query_heads.shape)
    )
    key_gradient = key_total.astype(jnp.bfloat16).reshape(key_heads.shape)
    value_gradient = value_total.astype(jnp.bfloat16).reshape(value_heads.shape)
    proj_grad = proj_part[None]
    gate_grad = gate_sum.astype(jnp.bfloat16)[None]
    up_grad = up_sum.astype(jnp.bfloat16)[None]
    down_grad = down_sum.astype(jnp.bfloat16)[None]
    return (
        query_gradient,
        key_gradient,
        value_gradient,
        hidden_grad,
        gain_grad,
        proj_grad,
        gate_grad,
        up_grad,
        down_grad,
    )


def solution(mesh):
    return jax.shard_map(
        on_device,
        mesh=mesh,
        in_specs=(
            P("exp", None, "ctx", "head", None),
            P("exp", None, "ctx", "head", None),
            P("exp", None, "ctx", "head", None),
            P("exp", "head", "ctx", None),
            P("exp", "head", "ctx", None),
            P(),
            P("exp", "head", "ctx", None),
            P("exp", "head", "ctx", None),
            P("head", None, None),
            P(("ctx", "head", "exp"), None, None),
            P(("ctx", "head", "exp"), None, None),
            P(("ctx", "head", "exp"), None, None),
        ),
        out_specs=(
            P("exp", None, "ctx", "head", None),
            P("exp", None, "ctx", "head", None),
            P("exp", None, "ctx", "head", None),
            P("exp", "head", "ctx", None),
            P(),
            P("head", ("ctx", "exp"), None),
            P(("ctx", "head", "exp"), None, None),
            P(("ctx", "head", "exp"), None, None),
            P(("ctx", "head", "exp"), None, None),
        ),
        check_vma=False,
    )
```

profile of v0, /device:TPU:0, one launch (start us, length us, event | category | flops | bytes accessed | tf_op | source)
XLA Modules:
  0.0 627.1 jit_solution(4999546773706749760)
XLA Ops:
  15.0 2.4 fusion.12
  17.4 4.1 pad
  21.5 6.7 %pad.1 = bf16[1024,4096]{1,0:T(8,128)(2,1)} pad(bf16[1024,2048]{1,0:T(8,128)(2,1)} %fusion.12, bf16[]{:T(256)} %constant.70), padding=0_0x2048_0 | pad | bytes 12582914 | tf_op jit(solution)/shard_map/concatenate | solution.py:89
  28.2 20.2 %scatter_custom_fusion = bf16[1152,4096]{1,0:T(8,128)(2,1)} fusion(s32[1024]{0:T(1024)S(1)} %bitcast.148, bf16[1024,4096]{1,0:T(8,128)(2,1)} %pad, bf16[1024,4096]{1,0:T(8,128)(2,1)} %pad.1, bf16[]{:T(256)} %constant.55.clone.1), kind=kCustom, calls=%fused_computation.23 | custom fusion | flops 4194304 | bytes 26214402 | tf_op jit(solution)/shard_map/scatter | solution.py:93
  48.4 13.2 %reshape.234 = bf16[32,36,4096]{2,1,0:T(8,128)(2,1)} reshape(bf16[1152,4096]{1,0:T(8,128)(2,1)} %scatter_custom_fusion) | data formatting | bytes 18874368 | tf_op jit(solution)/shard_map/reshape | solution.py:96
  61.5 236.4 %all_to_all.10 = bf16[32,36,4096]{2,1,0:T(8,128)(2,1)} all-to-all(bf16[32,36,4096]{2,1,0:T(8,128)(2,1)} %reshape.234), channel_id=1, replica_groups=mesh['ctx'=2,'head'=4,'exp'=4] {'ctx','head','exp'}, dimensions={0} | all-to-all | bytes 18874368 | tf_op jit(solution)/shard_map/all_to_all | solution.py:95
  298.0 13.3 %reshape.235 = bf16[1152,4096]{1,0:T(8,128)(2,1)} reshape(bf16[32,36,4096]{2,1,0:T(8,128)(2,1)} %all_to_all.10) | data formatting | bytes 18874368 | tf_op jit(solution)/shard_map/reshape | solution.py:103
  311.3 5.8 fusion.24
  317.3 5.6 fusion.27
  322.9 7.8 %multiply_convert_fusion.2 = (bf16[1152,768]{1,0:T(8,128)(2,1)}, bf16[1152,768]{1,0:T(8,128)(2,1)}) fusion(f32[1152,768]{1,0:T(8,128)S(1)} %fusion.24, f32[1152,768]{1,0:T(8,128)} %fusion.27, bf16[1,768,2048]{2,1,0:T(8,128)(2,1)S(1)} %copy-done.11, bf16[1152,4096]{1,0:T(8,128)(2,1)S(1)} %copy-done.2), kind=kOutput, calls=%fused_computation.36 | convolution fusion | flops 3635380224 | bytes 18481152 | tf_op jit(solution)/shard_map/dot_general | solution.py:34
  330.7 7.9 %fusion.22 = f32[1152,2048]{1,0:T(8,128)} fusion(bf16[1152,768]{1,0:T(8,128)(2,1)} %get-tuple-element.101, bf16[1,2048,768]{2,1,0:T(8,128)(2,1)S(1)} %copy-done), kind=kOutput, calls=%fused_computation.42 | convolution fusion | flops 3623878656 | bytes 14352384 | tf_op jit(solution)/shard_map/dot_general | solution.py:44
  338.6 8.0 %add_convert_fusion = bf16[1152,2048]{1,0:T(8,128)(2,1)} fusion(f32[1152,2048]{1,0:T(8,128)} %fusion.22, bf16[1152,768]{1,0:T(8,128)(2,1)S(1)} %copy-done.17, bf16[1,2048,768]{2,1,0:T(8,128)(2,1)S(1)} %copy-done.12), kind=kOutput, calls=%fused_computation.22 | convolution fusion | flops 3628597248 | bytes 19070976 | tf_op jit(solution)/shard_map/dot_general | solution.py:46
  346.6 7.2 %reshape.236 = bf16[32,36,2048]{2,1,0:T(8,128)(2,1)} reshape(bf16[1152,2048]{1,0:T(8,128)(2,1)} %add_convert_fusion) | data formatting | bytes 9437184 | tf_op jit(solution)/shard_map/reshape | solution.py:110
  353.8 3.6 all-to-all-start.1
  357.9 113.7 %all-to-all-done.1 = bf16[32,36,2048]{2,1,0:T(8,128)(2,1)} async-done(((bf16[32,36,2048]{2,1,0:T(8,128)(2,1)}), bf16[32,36,2048]{2,1,0:T(8,128)(2,1)}, u32[]{:S(2)}, u32[]{:S(2)}) %all-to-all-start.1) | async-done | bytes 4718624 | tf_op jit(solution)/shard_map/all_to_all | solution.py:109
  471.6 7.3 %reshape.237 = bf16[1152,2048]{1,0:T(8,128)(2,1)} reshape(bf16[32,36,2048]{2,1,0:T(8,128)(2,1)} %all-to-all-done.1) | data formatting | bytes 9437184 | tf_op jit(solution)/shard_map/reshape | solution.py:116
  478.9 11.8 %gather_fusion = bf16[1024,2048]{1,0:T(8,128)(2,1)} fusion(bf16[1152,2048]{1,0:T(8,128)(2,1)} %reshape.237, s32[1024]{0:T(1024)S(1)} %broadcast_clamp_fusion), kind=kCustom, calls=%fused_computation | custom fusion | bytes 8392704 | tf_op jit(solution)/shard_map/gather | solution.py:116
  490.7 5.1 convert_reduce_fusion
  497.7 2.0 all_gather.11
  499.7 2.0 all_gather.12
  501.7 6.4 %conditional.2 = (f32[4,512]{1,0:T(4,128)}, f32[4,512]{1,0:T(4,128)}, f32[4,512,128]{2,1,0:T(8,128)S(1)}, f32[4,512]{1,0:T(4,128)S(1)}) conditional(s32[]{:T(128)} %convert_element_type.142, () %tuple.30, (s32[512]{0:T(512)S(1)}, bf16[4,512,128]{2,1,0:T(8,128)(2,1)S(1)}, bf16[4,256,128]{2,1,0:T(8,128)(2,1)S(1)}, ...), branch_computations={%region_0.0_spmd, %region_1.4_spmd} | conditional | flops 944896000 | bytes 8980512 | solution.py:177
  504.7 2.7 fusion
  509.6 24.1 %all-gather.2.cloned.1.call-done = bf16[1,4,128,2048]{3,2,0,1:T(8,128)(2,1)} async-done(((bf16[1,1,128,2048]{3,2,0,1:T(8,128)(2,1)}), bf16[1,4,128,2048]{3,2,0,1:T(8,128)(2,1)}) %all-gather.2.cloned.1.call-update) | async-done | bytes 2097168 | tf_op jit(solution)/shard_map/all_gather | solution.py:182
  533.7 4.2 convolution_convert_fusion.2
  538.1 3.5 fusion.51
  541.9 7.1 %conditional.3 = (bf16[4,512,128]{2,1,0:T(8,128)(2,1)}, bf16[4,256,128]{2,1,0:T(8,128)(2,1)}, bf16[4,256,128]{2,1,0:T(8,128)(2,1)}) conditional(s32[]{:T(128)} %convert_element_type.142, () %tuple.29, (s32[512]{0:T(512)S(1)}, bf16[4,512,128]{2,1,0:T(8,128)(2,1)S(1)}, bf16[4,256,128]{2,1,0:T(8,128)(2,1)S(1)}, f32[4,512]{1,0:T(4,128)}, ...), branch_computations={%region_9.0_spmd, %region_10.12_spmd} | conditional | flops 676462592 | bytes 17352784 | solution.py:246
  549.7 9.0 %fusion.37 = bf16[1,2048,768]{2,1,0:T(8,128)(2,1)} fusion(bf16[1152,768]{1,0:T(8,128)(2,1)} %get-tuple-element.100, bf16[1152,4096]{1,0:T(8,128)(2,1)} %reshape.235), kind=kOutput, calls=%fused_computation.55 | convolution fusion | flops 3625451520 | bytes 9633792 | tf_op jit(solution)/shard_map/dot_general | solution.py:43
  558.7 8.3 %fusion.34 = bf16[1,2048,768]{2,1,0:T(8,128)(2,1)} fusion(bf16[1152,768]{1,0:T(8,128)(2,1)S(1)} %copy-done.16, bf16[1152,4096]{1,0:T(8,128)(2,1)} %reshape.235), kind=kOutput, calls=%fused_computation.54 | convolution fusion | flops 3625451520 | bytes 9633792 | tf_op jit(solution)/shard_map/dot_general | solution.py:42
  567.0 8.5 %fusion.40 = bf16[1,768,2048]{2,1,0:T(8,128)(2,1)} fusion(bf16[1152,4096]{1,0:T(8,128)(2,1)} %reshape.235, f32[1152,768]{1,0:T(8,128)S(1)} %copy-done.15, f32[1152,768]{1,0:T(8,128)S(1)} %copy-done.14), kind=kOutput, calls=%fused_computation.56 | convolution fusion | flops 3630759936 | bytes 14942208 | tf_op jit(solution)/shard_map/dot_general | solution.py:41
  575.5 40.6 %psum.7 = f32[2048]{0:T(1024)} all-reduce(f32[2048]{0:T(1024)S(1)} %get-tuple-element.94), channel_id=1, replica_groups=mesh['ctx'=2,'head'=4,'exp'=4] {'ctx','head','exp'}, use_global_device_ids=true, to_apply=%region_15.16 | all-reduce | flops 2048 | bytes 16384 | tf_op jit(solution)/shard_map/psum | solution.py:120
  616.0 2.2 copy.67
  618.3 2.0 convert_element_type.167
  (89 shorter events, 23.5 us)
Async XLA Ops:
  7.2 304.1 %copy-start = (bf16[1,2048,768]{2,1,0:T(8,128)(2,1)S(1)}, bf16[1,2048,768]{2,1,0:T(8,128)(2,1)}, u32[]{:S(2)}) copy-start(bf16[1,2048,768]{2,1,0:T(8,128)(2,1)} %param.25) | copy-start | bytes 9437188
  7.2 5.9 copy-start.10
  311.3 5.9 copy-start.2
  311.3 6.0 copy-start.12
  317.3 5.7 copy-start.13
  317.3 5.7 copy-start.11
  330.7 7.9 %copy-start.17 = (bf16[1152,768]{1,0:T(8,128)(2,1)S(1)}, bf16[1152,768]{1,0:T(8,128)(2,1)}, u32[]{:S(2)}) copy-start(bf16[1152,768]{1,0:T(8,128)(2,1)} %get-tuple-element.100) | copy-start | bytes 5308420
  353.8 117.8 %all-to-all-start.1 = ((bf16[32,36,2048]{2,1,0:T(8,128)(2,1)}), bf16[32,36,2048]{2,1,0:T(8,128)(2,1)}, u32[]{:S(2)}, u32[]{:S(2)}) async-start(bf16[32,36,2048]{2,1,0:T(8,128)(2,1)} %reshape.236), calls=%async_computation.1 | async-start | bytes 10485760 | tf_op jit(solution)/shard_map/all_to_all | solution.py:109
  357.4 176.3 %all-gather.2.cloned.1.call-start = ((), (), s32[]{:S(2)}) async-start(), calls=%async_computation.6 | async-start | bytes 2621440 | tf_op jit(solution)/shard_map/all_gather | solution.py:182
  490.7 5.1 copy-start.3
  490.7 5.5 copy-start.4
  495.8 1.7 copy-start.7
  495.8 1.9 copy-start.8
  495.8 3.9 copy-start.9
  497.4 61.3 %reduce-scatter.9.cloned.1.call-start = ((), (), s32[]{:S(2)}) async-start(), calls=%async_computation.9 | async-start | bytes 3145728 | tf_op jit(solution)/shard_map/reduce_scatter | solution.py:259
  537.9 82.4 %reduce-scatter.5.cloned.1.call-start = ((), (), s32[]{:S(2)}) async-start(), calls=%async_computation.7 | async-start | bytes 393216 | tf_op jit(solution)/shard_map/reduce_scatter | solution.py:253
  541.9 1.1 copy-start.5
  546.1 1.7 copy-start.6
  549.0 71.3 %reduce-scatter.7.cloned.1.call-start = ((), (), s32[]{:S(2)}) async-start(), calls=%async_computation.8 | async-start | bytes 393216 | tf_op jit(solution)/shard_map/reduce_scatter | solution.py:256
  549.6 9.1 %copy-start.16 = (bf16[1152,768]{1,0:T(8,128)(2,1)S(1)}, bf16[1152,768]{1,0:T(8,128)(2,1)}, u32[]{:S(2)}) copy-start(bf16[1152,768]{1,0:T(8,128)(2,1)} %get-tuple-element.101) | copy-start | bytes 5308420
  549.6 70.7 %reduce-scatter.11.cloned.1.call-start = ((), (), s32[]{:S(2)}) async-start(), calls=%async_computation.10 | async-start | bytes 1310720 | tf_op jit(solution)/shard_map/reduce_scatter | solution.py:263
  558.7 8.3 %copy-start.14 = (f32[1152,768]{1,0:T(8,128)S(1)}, f32[1152,768]{1,0:T(8,128)}, u32[]{:S(2)}) copy-start(f32[1152,768]{1,0:T(8,128)} %copy-done.13) | copy-start | bytes 10616836
  558.7 8.3 %copy-start.15 = (f32[1152,768]{1,0:T(8,128)S(1)}, f32[1152,768]{1,0:T(8,128)}, u32[]{:S(2)}) copy-start(f32[1152,768]{1,0:T(8,128)} %fusion.27) | copy-start | bytes 10616836
  567.0 53.3 %copy-start.1 = (bf16[1,2048,768]{2,1,0:T(8,128)(2,1)S(1)}, bf16[1,2048,768]{2,1,0:T(8,128)(2,1)}, u32[]{:S(2)}) copy-start(bf16[1,2048,768]{2,1,0:T(8,128)(2,1)} %param.25) | copy-start | bytes 9437188
Sparse Core Ops, SparseCore 0:
  497.5 36.1 all-gather.1
  538.0 9.5 reduce-scatter.8
  550.6 8.8 reduce-scatter.4
  562.1 8.7 reduce-scatter.6
  573.8 29.0 reduce-scatter.10
where the time goes:
time: 637 us; the launch traced here: 627 us
  blocking collectives  281 us (44%)
  waiting for transfers between devices  138 us (22%)
  matrix products  78.2 us (12%)
  local copies, waits for them, and re-layouts  72.3 us (11%)
  other arithmetic  38.5 us (6%)
  between operations  14.3 us (2%)
    all_to_all x1, blocking collectives, on_device(): lax.all_to_all(outbox.reshape(device_count, capacity, 2 * model_width), (...  236 us
    all_to_all x1, waiting for transfers between devices, on_device(): lax.all_to_all(back_rows.reshape(device_count, capacity, model_width), ('...  114 us
    psum x1, blocking collectives, on_device(): lax.psum(jnp.sum(normed_grad * unit_rows, axis=0), ('ctx', 'head', 'exp'))  40.6 us
    all_gather x1, waiting for transfers between devices, on_device(): grad_block = lax.all_gather(hidden_grad, 'head', axis=1, tiled=True)[0]  24.1 us
    scatter x1, other arithmetic, on_device(): jnp.zeros((device_count * capacity, 2 * model_width), jnp.bfloat16)  20.2 us
    reshape x1, local copies, waits for them, and re-layouts, on_device(): arrived.reshape(-1, 2 * model_width)  13.3 us
    reshape x1, local copies, waits for them, and re-layouts, on_device(): outbox.reshape(device_count, capacity, 2 * model_width)  13.2 us
  transfers between devices with their start and end apart: 6, of which 2 were waited for; matrix products, arithmetic and copies ran while one was open for 8% of the time, Pallas kernels for 0%

commit v1 on v0

--- a/solution.py
+++ b/solution.py
@@ -7,6 +7,9 @@
 FLOOR_SCORE = -1e30
 ROWS_DIMS = (((0,), (0,)), ((), ()))
 LAST_DIMS = (((1,), (1,)), ((), ()))
+HIDDEN_PIECES = 2
+GRAD_PIECES = 1
+BACK_PIECES = 2
 
 
 def slot_capacity(token_rows, choices, experts):
@@ -26,25 +29,36 @@
     return split_vals.transpose(0, 2, 1, 3).reshape(seq_count, block_len, per_key * head_size)
 
 
-def expert_backward(rows_in, gate_mat, up_mat, down_mat, model_width):
-    inputs = rows_in[:, :model_width]
-    upstream = rows_in[:, model_width:]
-    gate_val = jnp.dot(inputs, gate_mat, preferred_element_type=jnp.float32)
-    up_val = jnp.dot(inputs, up_mat, preferred_element_type=jnp.float32)
-    grad_act = lax.dot_general(upstream, down_mat, LAST_DIMS, preferred_element_type=jnp.float32)
-    sigma_gate = jax.nn.sigmoid(gate_val)
-    act_rows = (gate_val * sigma_gate * up_val).astype(jnp.bfloat16)
-    up_part = (grad_act * gate_val * sigma_gate).astype(jnp.bfloat16)
-    gate_part = (grad_act * up_val * sigma_gate * (1.0 + gate_val * (1.0 - sigma_gate))).astype(
-        jnp.bfloat16
-    )
-    down_sum = lax.dot_general(act_rows, upstream, ROWS_DIMS, preferred_element_type=jnp.float32)
-    gate_sum = lax.dot_general(inputs, gate_part, ROWS_DIMS, preferred_element_type=jnp.float32)
-    up_sum = lax.dot_general(inputs, up_part, ROWS_DIMS, preferred_element_type=jnp.float32)
-    back_rows = lax.dot_general(
-        gate_part, gate_mat, LAST_DIMS, preferred_element_type=jnp.float32
-    ) + lax.dot_general(up_part, up_mat, LAST_DIMS, preferred_element_type=jnp.float32)
-    return (back_rows.astype(jnp.bfloat16), gate_sum, up_sum, down_sum)
+def column_pieces(rows, pieces):
+    width = rows.shape[-1] // pieces
+    return [rows[..., i * width : (i + 1) * width] for i in range(pieces)]
+
+
+def direct_scatter(blocks, axis):
+    count = lax.axis_size(axis)
+    me = lax.axis_index(axis)
+    total = lax.dynamic_index_in_dim(blocks, me, 0, keepdims=False)
+    for step in range(1, count):
+        share = lax.dynamic_index_in_dim(blocks, (me + step) % count, 0, keepdims=False)
+        arrived = lax.ppermute(
+            share.astype(jnp.bfloat16), axis, [(i, (i + step) % count) for i in range(count)]
+        )
+        total = total + arrived.astype(jnp.float32)
+    return total
+
+
+def direct_gather(block, axis):
+    count = lax.axis_size(axis)
+    me = lax.axis_index(axis)
+    held = [block] + [
+        lax.ppermute(block, axis, [(i, (i + step) % count) for i in range(count)])
+        for step in range(1, count)
+    ]
+    stacked = jnp.stack(held)
+    return [
+        lax.dynamic_index_in_dim(stacked, (me - i) % count, 0, keepdims=False)
+        for i in range(count)
+    ]
 
 
 def on_device(
@@ -65,59 +79,108 @@
     token_rows = hidden_state.shape[2]
     choices = expert_ids.shape[-1]
     device_count = lax.axis_size(("ctx", "head", "exp"))
-    capacity = slot_capacity(token_rows, choices, device_count)
-    hidden_wide = hidden_state.reshape(token_rows, model_width).astype(jnp.float32)
+    exp_count = lax.axis_size("exp")
+    plane_count = device_count // exp_count
+    capacity = slot_capacity(token_rows, choices, device_count) * exp_count
+    group_rows = exp_count * token_rows
+    own_hidden = hidden_state.reshape(token_rows, model_width)
     out_rows = output_grad.reshape(token_rows, model_width)
+    hidden_wide = own_hidden.astype(jnp.float32)
     inv_rms = lax.rsqrt(jnp.mean(hidden_wide * hidden_wide, axis=1, keepdims=True) + NORM_EPS)
     unit_rows = hidden_wide * inv_rms
-    normed = (unit_rows * norm_gain).astype(jnp.bfloat16)
-    probs_flat = gate_probs.reshape(token_rows, choices)
-    expert_grad = (probs_flat[:, :, None] * out_rows.astype(jnp.float32)[:, None, :]).astype(
+    routing = jnp.concatenate(
+        [
+            expert_ids.reshape(token_rows, choices).astype(jnp.float32),
+            gate_probs.reshape(token_rows, choices),
+            inv_rms,
+        ],
+        axis=1,
+    )
+    group_routing = lax.all_gather(routing, "exp", axis=0, tiled=True)
+    group_hidden = [
+        lax.all_gather(piece, "exp", axis=0, tiled=True)
+        for piece in column_pieces(own_hidden, HIDDEN_PIECES)
+    ]
+    group_grad = [
+        lax.all_gather(piece, "exp", axis=0, tiled=True)
+        for piece in column_pieces(out_rows, GRAD_PIECES)
+    ]
+    group_rms = group_routing[:, 2 * choices :]
+
+    plane_experts = jnp.arange(plane_count, dtype=jnp.int32) * exp_count + lax.axis_index("exp")
+    group_ids = group_routing[:, :choices].astype(jnp.int32)
+    names = (group_ids[None, :, :] == plane_experts[:, None, None]).astype(jnp.float32)
+    named = jnp.sum(names, axis=2)
+    named_prob = jnp.sum(names * group_routing[None, :, choices : 2 * choices], axis=2)
+    earlier = (jnp.arange(group_rows)[:, None] < jnp.arange(group_rows)[None, :]).astype(
         jnp.bfloat16
     )
-    flat_ids = expert_ids.reshape(-1)
-    pick_count = flat_ids.shape[0]
-    chosen = (flat_ids[:, None] == jnp.arange(device_count, dtype=jnp.int32)[None, :]).astype(
+    before = jnp.dot(named.astype(jnp.bfloat16), earlier, preferred_element_type=jnp.float32)
+    slot_of = jnp.where(named > 0.0, before, -1.0)
+    picks = slot_of[:, None, :] == jnp.arange(capacity, dtype=jnp.float32)[None, :, None]
+    slot_prob = jnp.sum(jnp.where(picks, named_prob[:, None, :], 0.0), axis=2).reshape(-1, 1)
+    picker = picks.astype(jnp.bfloat16).reshape(plane_count * capacity, group_rows)
+
+    def exchange(rows):
+        return lax.all_to_all(rows, ("ctx", "head"), split_axis=0, concat_axis=0, tiled=True)
+
+    def pick(rows):
+        return jnp.dot(picker, rows, preferred_element_type=jnp.float32)
+
+    inputs = []
+    for piece, gain in zip(group_hidden, column_pieces(norm_gain, HIDDEN_PIECES)):
+        normed = (piece.astype(jnp.float32) * group_rms * gain).astype(jnp.bfloat16)
+        inputs.append(exchange(pick(normed).astype(jnp.bfloat16)))
+    upstream = [exchange((pick(piece) * slot_prob).astype(jnp.bfloat16)) for piece in group_grad]
+
+    gate_mat, up_mat, down_mat = (gate_weight[0], up_weight[0], down_weight[0])
+    x_width = model_width // HIDDEN_PIECES
+    gate_val = up_val = grad_act = 0.0
+    for i, piece in enumerate(inputs):
+        rows = slice(i * x_width, (i + 1) * x_width)
+        gate_val += jnp.dot(piece, gate_mat[rows], preferred_element_type=jnp.float32)
+        up_val += jnp.dot(piece, up_mat[rows], preferred_element_type=jnp.float32)
+    for piece, mat in zip(upstream, column_pieces(down_mat, GRAD_PIECES)):
+        grad_act += lax.dot_general(piece, mat, LAST_DIMS, preferred_element_type=jnp.float32)
+    sigma_gate = jax.nn.sigmoid(gate_val)
+    act_rows = (gate_val * sigma_gate * up_val).astype(jnp.bfloat16)
+    up_part = (grad_act * gate_val * sigma_gate).astype(jnp.bfloat16)
+    gate_part = (grad_act * up_val * sigma_gate * (1.0 + gate_val * (1.0 - sigma_gate))).astype(
         jnp.bfloat16
     )
-    earlier = (jnp.arange(pick_count)[:, None] > jnp.arange(pick_count)[None, :]).astype(
-        jnp.bfloat16
-    )
-    before = jnp.dot(earlier, chosen, preferred_element_type=jnp.float32)
-    slot_pos = jnp.sum(before * chosen.astype(jnp.float32), axis=1).astype(jnp.int32)
-    target = flat_ids * capacity + slot_pos
-    payload = jnp.concatenate(
-        [jnp.repeat(normed, choices, axis=0), expert_grad.reshape(pick_count, model_width)], axis=1
-    )
-    outbox = (
-        jnp.zeros((device_count * capacity, 2 * model_width), jnp.bfloat16).at[target].set(payload)
-    )
-    arrived = lax.all_to_all(
-        outbox.reshape(device_count, capacity, 2 * model_width),
-        ("ctx", "head", "exp"),
-        split_axis=0,
-        concat_axis=0,
-        tiled=True,
-    )
-    back_rows, gate_sum, up_sum, down_sum = expert_backward(
-        arrived.reshape(-1, 2 * model_width),
-        gate_weight[0],
-        up_weight[0],
-        down_weight[0],
-        model_width,
-    )
-    returned = lax.all_to_all(
-        back_rows.reshape(device_count, capacity, model_width),
-        ("ctx", "head", "exp"),
-        split_axis=0,
-        concat_axis=0,
-        tiled=True,
-    )
-    picked_back = returned.reshape(device_count * capacity, model_width)[target]
-    normed_grad = jnp.sum(
-        picked_back.reshape(token_rows, choices, model_width).astype(jnp.float32), axis=1
-    )
-    gain_grad = lax.psum(jnp.sum(normed_grad * unit_rows, axis=0), ("ctx", "head", "exp"))
+    back_width = model_width // BACK_PIECES
+    normed_pieces = []
+    for i in range(BACK_PIECES):
+        rows = slice(i * back_width, (i + 1) * back_width)
+        back_rows = lax.dot_general(
+            gate_part, gate_mat[rows], LAST_DIMS, preferred_element_type=jnp.float32
+        ) + lax.dot_general(up_part, up_mat[rows], LAST_DIMS, preferred_element_type=jnp.float32)
+        returned = exchange(back_rows.astype(jnp.bfloat16))
+        group_back = lax.dot_general(
+            picker, returned, ROWS_DIMS, preferred_element_type=jnp.float32
+        ).astype(jnp.bfloat16)
+        normed_pieces.append(
+            lax.psum_scatter(group_back, "exp", scatter_dimension=0, tiled=True)
+        )
+    all_inputs = jnp.concatenate(inputs, axis=1)
+    all_upstream = jnp.concatenate(upstream, axis=1)
+    down_grad = lax.dot_general(
+        act_rows, all_upstream, ROWS_DIMS, preferred_element_type=jnp.float32
+    ).astype(jnp.bfloat16)[None]
+    gate_grad = lax.dot_general(
+        all_inputs, gate_part, ROWS_DIMS, preferred_element_type=jnp.float32
+    ).astype(jnp.bfloat16)[None]
+    up_grad = lax.dot_general(
+        all_inputs, up_part, ROWS_DIMS, preferred_element_type=jnp.float32
+    ).astype(jnp.bfloat16)[None]
+    normed_pieces, down_grad, gate_grad, up_grad = lax.optimization_barrier(
+        (normed_pieces, down_grad, gate_grad, up_grad)
+    )
+    normed_grad = jnp.concatenate(normed_pieces, axis=1).astype(jnp.float32)
+    gain_terms = jnp.sum(normed_grad * unit_rows, axis=0)
+    for axis in ("ctx", "head", "exp"):
+        gain_terms = sum(direct_gather(gain_terms, axis))
+    gain_grad = gain_terms
     scaled = normed_grad * norm_gain
     mixed_term = jnp.mean(scaled * unit_rows, axis=1, keepdims=True)
     hidden_rows = (
@@ -174,13 +237,10 @@
         )
         return (new_max, new_sum, new_acc)
 
-    run_max, run_sum, run_acc = lax.cond(
-        jnp.int32(0) <= query_last, forward_update, lambda current: current, initial
-    )
+    run_max, run_sum, run_acc = forward_update(initial)
     log_sum = run_max + jnp.log(run_sum)
     attn_rows = (run_acc / run_sum[:, :, None]).astype(jnp.bfloat16)
-    grad_block = lax.all_gather(hidden_grad, "head", axis=1, tiled=True)[0]
-    grad_tokens = grad_block.reshape(seq_count * block_len, model_width)
+    grad_tokens = jnp.concatenate(direct_gather(hidden_rows, "head"), axis=0)
     proj_mat = out_weight[0]
     attn_grad_tok = lax.dot_general(
         grad_tokens, proj_mat, LAST_DIMS, preferred_element_type=jnp.float32
@@ -199,15 +259,9 @@
         jnp.zeros((seq_count, seq_len, head_size), jnp.float32),
         jnp.zeros((seq_count, seq_len, head_size), jnp.float32),
     )
-    pieces = (
-        lax.all_gather(key_heads, "ctx", axis=2, tiled=True),
-        lax.all_gather(value_heads, "ctx", axis=2, tiled=True),
-    )
-    backward_key_piece = pieces[0][0, :, :, 0, :]
-    backward_value_piece = pieces[1][0, :, :, 0, :]
 
     def backward_update(current):
-        attention_scores, allowed = piece_scores(backward_key_piece)
+        attention_scores, allowed = piece_scores(key_piece)
         probability_values = jnp.where(
             allowed, jnp.exp(attention_scores - log_sum[:, :, None]), 0.0
         )
@@ -220,7 +274,7 @@
         probability_gradient = jnp.einsum(
             "sqd,skd->sqk",
             attention_gradient,
-            backward_value_piece,
+            value_piece,
             preferred_element_type=jnp.float32,
         )
         score_gradient = (
@@ -230,7 +284,7 @@
             jnp.einsum(
                 "sqk,skd->sqd",
                 score_gradient,
-                backward_key_piece,
+                key_piece,
                 preferred_element_type=jnp.float32,
             )
             * score_scaling
@@ -243,35 +297,28 @@
         )
         return (query_acc, key_part, value_part)
 
-    query_acc, key_acc, value_acc = lax.cond(
-        jnp.int32(0) <= query_last, backward_update, lambda current: current, initial_grads
-    )
+    query_acc, key_acc, value_acc = backward_update(initial_grads)
     proj_full = lax.dot_general(
         attn_tokens, grad_tokens, ROWS_DIMS, preferred_element_type=jnp.float32
     )
-    key_total, value_total, proj_mid = (
-        lax.psum_scatter(
-            key_acc.astype(jnp.bfloat16), "ctx", scatter_dimension=1, tiled=True
-        ).astype(jnp.float32),
-        lax.psum_scatter(
-            value_acc.astype(jnp.bfloat16), "ctx", scatter_dimension=1, tiled=True
-        ).astype(jnp.float32),
-        lax.psum_scatter(
-            proj_full.astype(jnp.bfloat16), "ctx", scatter_dimension=0, tiled=True
-        ).astype(jnp.float32),
-    )
-    proj_part = lax.psum_scatter(
-        proj_mid.astype(jnp.bfloat16), "exp", scatter_dimension=0, tiled=True
-    )
+    def by_position(terms):
+        return terms.reshape(seq_count, ctx_count, block_len, head_size).transpose(1, 0, 2, 3)
+
+    exp_rows = proj_full.shape[0] // (ctx_count * exp_count)
+    proj_mid = direct_scatter(
+        proj_full.reshape(ctx_count, exp_count * exp_rows, model_width), "ctx"
+    )
+    proj_part = direct_scatter(proj_mid.reshape(exp_count, exp_rows, model_width), "exp").astype(
+        jnp.bfloat16
+    )
+    key_total = direct_scatter(by_position(key_acc), "ctx")
+    value_total = direct_scatter(by_position(value_acc), "ctx")
     query_gradient = (
         rows_to_heads(query_acc, per_key, block_len).astype(jnp.bfloat16).reshape(query_heads.shape)
     )
     key_gradient = key_total.astype(jnp.bfloat16).reshape(key_heads.shape)
     value_gradient = value_total.astype(jnp.bfloat16).reshape(value_heads.shape)
     proj_grad = proj_part[None]
-    gate_grad = gate_sum.astype(jnp.bfloat16)[None]
-    up_grad = up_sum.astype(jnp.bfloat16)[None]
-    down_grad = down_sum.astype(jnp.bfloat16)[None]
     return (
         query_gradient,
         key_gradient,

time: 637 us -> 392 us (0.62)
  blocking collectives: 281 us -> 19.1 us
  local copies, waits for them, and re-layouts: 72.3 us -> 13 us
  waiting for transfers between devices: 138 us -> 187 us
  starting transfers between devices: 4.36 us -> 35.3 us
  other arithmetic: 38.5 us -> 15.6 us
  matrix products: 78.2 us -> 100 us
    all_to_all x1 -> x0, blocking collectives: 236 us -> none  [on_device(): lax.all_to_all(outbox.reshape(device_count, capacity, 2 * model_width), (...]
    all_gather x1 -> x3, waiting for transfers between devices: 24.1 us -> 65.8 us  [on_device(): lax.all_gather(piece, 'exp', axis=0, tiled=True)]
    reshape x5 -> x0, local copies, waits for them, and re-layouts: 41.6 us -> none  [the longest x1 13.3 us: on_device(): arrived.reshape(-1, 2 * model_width)]
    ppermute x0 -> x16, waiting for transfers between devices: none -> 40.7 us  [the longest x6 20.8 us: direct_scatter(): lax.ppermute(share.astype(jnp.bfloat16), axis, [(i, (i + step) % count) f...]
    psum x1 -> x0, blocking collectives: 40.6 us -> none  [on_device(): lax.psum(jnp.sum(normed_grad * unit_rows, axis=0), ('ctx', 'head', 'exp'))]
    all_to_all x1 -> x5, waiting for transfers between devices: 114 us -> 78.5 us  [exchange(): lax.all_to_all(rows, ('ctx', 'head'), split_axis=0, concat_axis=0, tiled=...]
    dot_general x11 -> x20, matrix products: 63.1 us -> 90.4 us  [the longest x3 15.2 us: pick(): return jnp.dot(picker, rows, preferred_element_type=jnp.float32)]
    scatter x1 -> x0, other arithmetic: 20.2 us -> none  [on_device(): jnp.zeros((device_count * capacity, 2 * model_width), jnp.bfloat16)]
  transfers between devices with their start and end apart: 6 -> 26, of which waited for: 2 -> 16; matrix products, arithmetic and copies ran while one was open for 8% -> 25% of each run, Pallas kernels for 0% -> 0%
where the time goes in v1:
time: 392 us; the launch traced here: 385 us
  waiting for transfers between devices  187 us (48%)
  matrix products  100 us (26%)
  starting transfers between devices  35.3 us (9%)
  blocking collectives  19.1 us (5%)
  other arithmetic  15.6 us (4%)
  between operations  14.9 us (4%)
  local copies, waits for them, and re-layouts  13 us (3%)
    all_to_all x5, waiting for transfers between devices, exchange(): lax.all_to_all(rows, ('ctx', 'head'), split_axis=0, concat_axis=0, tiled=...  78.5 us
    all_gather x3, waiting for transfers between devices, on_device(): lax.all_gather(piece, 'exp', axis=0, tiled=True)  65.8 us
    all_to_all x5, starting transfers between devices, exchange(): lax.all_to_all(rows, ('ctx', 'head'), split_axis=0, concat_axis=0, tiled=...  22 us
    ppermute x6, waiting for transfers between devices, direct_scatter(): lax.ppermute(share.astype(jnp.bfloat16), axis, [(i, (i + step) % count) f...  20.8 us
    ppermute x10, waiting for transfers between devices, direct_gather(): lax.ppermute(block, axis, [(i, (i + step) % count) for i in range(count)])  19.9 us
    dot_general x3, matrix products, pick(): return jnp.dot(picker, rows, preferred_element_type=jnp.float32)  15.2 us
    all_gather x1, blocking collectives, on_device(): group_routing = lax.all_gather(routing, 'exp', axis=0, tiled=True)  15 us
    dot_general x2, matrix products, on_device(): jnp.dot(piece, gate_mat[rows], preferred_element_type=jnp.float32)  9.86 us
  transfers between devices with their start and end apart: 26, of which 16 were waited for; matrix products, arithmetic and copies ran while one was open for 25% of the time, Pallas kernels for 0%

profile of v1, /device:TPU:0, one launch (start us, length us, event | category | flops | bytes accessed | tf_op | source)
XLA Modules:
  0.0 384.7 jit_solution(8969131948537852048)
XLA Ops:
  13.3 15.0 %all_gather.19 = f32[512,17]{0,1:T(8,128)S(1)} all-gather(f32[128,17]{0,1:T(8,128)S(1)} %pad_maximum_fusion.14), channel_id=1, replica_groups=mesh['ctx'=2,'head'=4,'exp'=4] {'exp'}, dimensions={0}, use_global_device_ids=true | all-gather | bytes 43520 | tf_op jit(solution)/shard_map/all_gather | solution.py:99
  29.9 11.2 %all-gather.7.cloned.1.call-done = bf16[512,1024]{1,0:T(8,128)(2,1)} async-done(((bf16[128,1024]{1,0:T(8,128)(2,1)}), bf16[512,1024]{1,0:T(8,128)(2,1)}) %all-gather.7.cloned.1.call-update) | async-done | bytes 1048592 | tf_op jit(solution)/shard_map/all_gather | solution.py:101
  41.1 4.3 %convolution_convert_fusion = bf16[1152,1024]{1,0:T(8,128)(2,1)} fusion(pred[1152,512]{1,0:T(32,128)(4,1)} %bitcast_compare_fusion, bf16[512,1024]{1,0:T(8,128)(2,1)} %all-gather.7.cloned.1.call-done, f32[1024]{0:T(1024)S(1)} %get-tuple-element.36, f32[512]{0:T(512)S(1)} %bitcast.280), kind=kOutput, calls=%fused_computation.7 | convolution fusion | flops 1211236352 | bytes 4003840 | tf_op jit(solution)/shard_map/dot_general | solution.py:128
  45.4 4.4 %all-to-all-start.2 = ((bf16[8,144,1024]{2,1,0:T(8,128)(2,1)}), bf16[8,144,1024]{2,1,0:T(8,128)(2,1)}, u32[]{:S(2)}, u32[]{:S(2)}) async-start(bf16[8,144,1024]{2,1,0:T(8,128)(2,1)} %bitcast.244), calls=%async_computation.2 | async-start | bytes 4718592 | tf_op jit(solution)/shard_map/all_to_all | solution.py:125
  50.5 20.3 %all-gather.5.cloned.1.call-done = bf16[512,1024]{1,0:T(8,128)(2,1)} async-done(((bf16[128,1024]{1,0:T(8,128)(2,1)}), bf16[512,1024]{1,0:T(8,128)(2,1)}) %all-gather.5.cloned.1.call-update) | async-done | bytes 1048592 | tf_op jit(solution)/shard_map/all_gather | solution.py:101
  70.8 4.3 %convolution_convert_fusion.1 = bf16[1152,1024]{1,0:T(8,128)(2,1)} fusion(pred[1152,512]{1,0:T(32,128)(4,1)} %bitcast_compare_fusion, bf16[512,1024]{1,0:T(8,128)(2,1)} %all-gather.5.cloned.1.call-done, f32[1024]{0:T(1024)S(1)} %get-tuple-element.37, f32[512]{0:T(512)S(1)} %bitcast.281), kind=kOutput, calls=%fused_computation.8 | convolution fusion | flops 1211236352 | bytes 4003840 | tf_op jit(solution)/shard_map/dot_general | solution.py:128
  75.2 3.6 all-to-all-done.2
  78.7 4.4 %all-to-all-start.1 = ((bf16[8,144,1024]{2,1,0:T(8,128)(2,1)}), bf16[8,144,1024]{2,1,0:T(8,128)(2,1)}, u32[]{:S(2)}, u32[]{:S(2)}) async-start(bf16[8,144,1024]{2,1,0:T(8,128)(2,1)} %bitcast.243), calls=%async_computation.1 | async-start | bytes 4718592 | tf_op jit(solution)/shard_map/all_to_all | solution.py:125
  83.6 34.3 %all-gather.9.cloned.1.call-done = bf16[1,1,512,2048]{3,2,1,0:T(8,128)(2,1)} async-done(((bf16[1,1,128,2048]{3,2,1,0:T(8,128)(2,1)}), bf16[1,1,512,2048]{3,2,1,0:T(8,128)(2,1)}) %all-gather.9.cloned.1.call-update) | async-done | bytes 2097168 | tf_op jit(solution)/shard_map/all_gather | solution.py:105
  117.9 6.6 %fusion = bf16[1152,2048]{1,0:T(8,128)(2,1)} fusion(pred[1152,512]{1,0:T(32,128)(4,1)} %bitcast_compare_fusion, f32[1152]{0:T(1024)S(1)} %mul.218, bf16[1,1,512,2048]{3,2,1,0:T(8,128)(2,1)} %all-gather.9.cloned.1.call-done), kind=kOutput, calls=%fused_computation.1 | convolution fusion | flops 2420637696 | bytes 7410176 | tf_op jit(solution)/shard_map/dot_general | solution.py:128
  124.5 4.8 %all-to-all-start = ((bf16[8,144,2048]{2,1,0:T(8,128)(2,1)}), bf16[8,144,2048]{2,1,0:T(8,128)(2,1)}, u32[]{:S(2)}, u32[]{:S(2)}) async-start(bf16[8,144,2048]{2,1,0:T(8,128)(2,1)} %bitcast.236), calls=%async_computation | async-start | bytes 9437184 | tf_op jit(solution)/shard_map/all_to_all | solution.py:125
  129.3 4.3 %fusion.22 = f32[1152,768]{1,0:T(8,128)S(1)} fusion(bf16[1152,1024]{1,0:T(8,128)(2,1)} %bitcast.17, bf16[1,2048,768]{2,1,0:T(8,128)(2,1)} %param.21), kind=kOutput, calls=%fused_computation.52 | convolution fusion | flops 1811939328 | bytes 7471104 | tf_op jit(solution)/shard_map/dot_general | solution.py:141
  133.6 3.8 fusion.27
  137.4 5.6 %convolution_add_fusion = f32[1152,768]{1,0:T(8,128)} fusion(f32[1152,768]{1,0:T(8,128)S(1)} %fusion.22, bf16[1152,1024]{1,0:T(8,128)(2,1)} %bitcast.20, bf16[1,2048,768]{2,1,0:T(8,128)(2,1)S(1)} %copy-done.30), kind=kOutput, calls=%fused_computation.5 | convolution fusion | flops 1812824064 | bytes 11010048 | tf_op jit(solution)/shard_map/dot_general | solution.py:141
  143.0 5.5 %convolution_add_fusion.1 = f32[1152,768]{1,0:T(8,128)} fusion(f32[1152,768]{1,0:T(8,128)S(1)} %fusion.27, bf16[1152,1024]{1,0:T(8,128)(2,1)} %bitcast.20, bf16[1,2048,768]{2,1,0:T(8,128)(2,1)S(1)} %copy-done.32), kind=kOutput, calls=%fused_computation.6 | convolution fusion | flops 1812824064 | bytes 11010048 | tf_op jit(solution)/shard_map/dot_general | solution.py:142
  148.5 35.0 %all-to-all-done = bf16[8,144,2048]{2,1,0:T(8,128)(2,1)} async-done(((bf16[8,144,2048]{2,1,0:T(8,128)(2,1)}), bf16[8,144,2048]{2,1,0:T(8,128)(2,1)}, u32[]{:S(2)}, u32[]{:S(2)}) %all-to-all-start) | async-done | bytes 4718624 | tf_op jit(solution)/shard_map/all_to_all | solution.py:125
  183.5 8.4 %multiply_convert_fusion.1 = (bf16[1152,768]{1,0:T(8,128)(2,1)S(1)}, bf16[1152,768]{1,0:T(8,128)(2,1)S(1)}) fusion(f32[1152,768]{1,0:T(8,128)} %convolution_add_fusion, f32[1152,768]{1,0:T(8,128)} %convolution_add_fusion.1, bf16[1152,2048]{1,0:T(8,128)(2,1)} %bitcast.13, bf16[1,768,2048]{2,1,0:T(8,128)(2,1)S(1)} %copy-done), kind=kOutput, calls=%fused_computation.10 | convolution fusion | flops 3635380224 | bytes 18481152 | tf_op jit(solution)/shard_map/dot_general | solution.py:144
  198.5 4.1 %all-to-all-start.4 = ((bf16[8,144,1024]{2,1,0:T(8,128)(2,1)}), bf16[8,144,1024]{2,1,0:T(8,128)(2,1)S(1)}, u32[]{:S(2)}, u32[]{:S(2)}) async-start(bf16[8,144,1024]{2,1,0:T(8,128)(2,1)} %bitcast.245), calls=%async_computation.5 | async-start | bytes 4718592 | tf_op jit(solution)/shard_map/all_to_all | solution.py:125
  202.6 4.1 %fusion.20 = f32[1152,1024]{1,0:T(8,128)S(1)} fusion(bf16[1152,768]{1,0:T(8,128)(2,1)} %copy-done.38, bf16[1,2048,768]{2,1,0:T(8,128)(2,1)} %param.21), kind=kOutput, calls=%fused_computation.50 | convolution fusion | flops 1811939328 | bytes 8060928 | tf_op jit(solution)/shard_map/dot_general | solution.py:155
  206.8 3.4 add_convert_fusion.1
  210.2 21.2 %all-to-all-done.4 = bf16[8,144,1024]{2,1,0:T(8,128)(2,1)S(1)} async-done(((bf16[8,144,1024]{2,1,0:T(8,128)(2,1)}), bf16[8,144,1024]{2,1,0:T(8,128)(2,1)S(1)}, u32[]{:S(2)}, u32[]{:S(2)}) %all-to-all-start.4) | async-done | bytes 2359328 | tf_op jit(solution)/shard_map/all_to_all | solution.py:125
  231.5 4.4 %all-to-all-start.3 = ((bf16[8,144,1024]{2,1,0:T(8,128)(2,1)}), bf16[8,144,1024]{2,1,0:T(8,128)(2,1)}, u32[]{:S(2)}, u32[]{:S(2)}) async-start(bf16[8,144,1024]{2,1,0:T(8,128)(2,1)} %bitcast.24), calls=%async_computation.3 | async-start | bytes 4718592 | tf_op jit(solution)/shard_map/all_to_all | solution.py:125
  246.0 18.8 %all-to-all-done.3 = bf16[8,144,1024]{2,1,0:T(8,128)(2,1)} async-done(((bf16[8,144,1024]{2,1,0:T(8,128)(2,1)}), bf16[8,144,1024]{2,1,0:T(8,128)(2,1)}, u32[]{:S(2)}, u32[]{:S(2)}) %all-to-all-start.3) | async-done | bytes 2359328 | tf_op jit(solution)/shard_map/all_to_all | solution.py:125
  264.8 4.2 %bitcast_convert_fusion.1 = bf16[512,1024]{1,0:T(8,128)(2,1)} fusion(bf16[8,144,1024]{2,1,0:T(8,128)(2,1)} %all-to-all-done.3, f32[8,512]{1,0:T(8,128)S(1)} %copy-done.25), kind=kOutput, calls=%fused_computation.34 | convolution fusion | flops 1209073664 | bytes 3424256 | tf_op jit(solution)/shard_map/dot_general | solution.py:159
  269.1 9.0 %fusion.5 = bf16[1,2048,768]{2,1,0:T(8,128)(2,1)} fusion(bf16[1152,768]{1,0:T(8,128)(2,1)} %copy-done.40, bf16[1152,1024]{1,0:T(8,128)(2,1)} %bitcast.20, bf16[1152,1024]{1,0:T(8,128)(2,1)} %bitcast.17), kind=kOutput, calls=%fused_computation.20 | convolution fusion | flops 3634888704 | bytes 9633792 | tf_op jit(solution)/shard_map/dot_general | solution.py:173
  278.1 8.6 %fusion.4 = bf16[1,2048,768]{2,1,0:T(8,128)(2,1)} fusion(bf16[1152,768]{1,0:T(8,128)(2,1)S(1)} %copy-done.39, bf16[1152,1024]{1,0:T(8,128)(2,1)} %bitcast.20, bf16[1152,1024]{1,0:T(8,128)(2,1)} %bitcast.17), kind=kOutput, calls=%fused_computation.19 | convolution fusion | flops 3634888704 | bytes 9633792 | tf_op jit(solution)/shard_map/dot_general | solution.py:170
  286.8 8.6 %fusion.3 = bf16[1,768,2048]{2,1,0:T(8,128)(2,1)} fusion(bf16[1152,2048]{1,0:T(8,128)(2,1)} %bitcast.13, f32[1152,768]{1,0:T(8,128)S(1)} %copy-done.37, f32[1152,768]{1,0:T(8,128)S(1)} %copy-done.36), kind=kOutput, calls=%fused_computation.18 | convolution fusion | flops 3630759936 | bytes 14942208 | tf_op jit(solution)/shard_map/dot_general | solution.py:167
  317.8 11.6 %collective-permute-done.1 = bf16[128,2048]{1,0:T(8,128)(2,1)S(1)} collective-permute-done((bf16[128,2048]{1,0:T(8,128)(2,1)S(1)}, bf16[128,2048]{1,0:T(8,128)(2,1)S(1)}, u32[]{:S(2)}, u32[]{:S(2)}) %collective-permute-start.1) | collective-permute-done | bytes 524320 | tf_op jit(solution)/shard_map/ppermute | solution.py:54
  351.1 3.8 collective-permute-start.15
  356.3 5.8 %collective-permute-done.13 = bf16[64,2048]{1,0:T(8,128)(2,1)S(1)} collective-permute-done((bf16[64,2048]{1,0:T(8,128)(2,1)S(1)}, bf16[64,2048]{1,0:T(8,128)(2,1)S(1)}, u32[]{:S(2)}, u32[]{:S(2)}) %collective-permute-start.13) | collective-permute-done | bytes 262176 | tf_op jit(solution)/shard_map/ppermute | solution.py:43
  362.1 3.4 collective-permute-done.15
  365.6 11.5 %collective-permute-done.14 = bf16[64,2048]{1,0:T(8,128)(2,1)S(1)} collective-permute-done((bf16[64,2048]{1,0:T(8,128)(2,1)S(1)}, bf16[64,2048]{1,0:T(8,128)(2,1)S(1)}, u32[]{:S(2)}, u32[]{:S(2)}) %collective-permute-start.14) | collective-permute-done | bytes 262176 | tf_op jit(solution)/shard_map/ppermute | solution.py:43
  (189 shorter events, 71.2 us)
Async XLA Ops:
  7.2 176.3 %copy-start = (bf16[1,768,2048]{2,1,0:T(8,128)(2,1)S(1)}, bf16[1,768,2048]{2,1,0:T(8,128)(2,1)}, u32[]{:S(2)}) copy-start(bf16[1,768,2048]{2,1,0:T(8,128)(2,1)} %param.23) | copy-start | bytes 9437188
  7.2 22.7 %copy-start.21 = (f32[2048]{0:T(1024)S(1)}, f32[2048]{0:T(1024)}, u32[]{:S(2)}) copy-start(f32[2048]{0:T(1024)} %param.17) | copy-start | bytes 24580
  7.2 33.9 %all-gather.7.cloned.1.call-start = ((), (), s32[]{:S(2)}) async-start(), calls=%async_computation.8 | async-start | bytes 1310720 | tf_op jit(solution)/shard_map/all_gather | solution.py:101
  9.3 61.6 %all-gather.5.cloned.1.call-start = ((), (), s32[]{:S(2)}) async-start(), calls=%async_computation.7 | async-start | bytes 1310720 | tf_op jit(solution)/shard_map/all_gather | solution.py:101
  28.6 207.3 %copy-start.24 = (f32[8,512]{1,0:T(8,128)}, f32[8,512]{1,0:T(8,128)S(1)}, u32[]{:S(2)}) copy-start(f32[8,512]{1,0:T(8,128)S(1)} %convolution_select_fusion) | copy-start | bytes 49156
  45.4 33.3 %all-to-all-start.2 = ((bf16[8,144,1024]{2,1,0:T(8,128)(2,1)}), bf16[8,144,1024]{2,1,0:T(8,128)(2,1)}, u32[]{:S(2)}, u32[]{:S(2)}) async-start(bf16[8,144,1024]{2,1,0:T(8,128)(2,1)} %bitcast.244), calls=%async_computation.2 | async-start | bytes 4718592 | tf_op jit(solution)/shard_map/all_to_all | solution.py:125
  49.8 68.1 %all-gather.9.cloned.1.call-start = ((), (), s32[]{:S(2)}) async-start(), calls=%async_computation.11 | async-start | bytes 2621440 | tf_op jit(solution)/shard_map/all_gather | solution.py:105
  78.7 45.7 %all-to-all-start.1 = ((bf16[8,144,1024]{2,1,0:T(8,128)(2,1)}), bf16[8,144,1024]{2,1,0:T(8,128)(2,1)}, u32[]{:S(2)}, u32[]{:S(2)}) async-start(bf16[8,144,1024]{2,1,0:T(8,128)(2,1)} %bitcast.243), calls=%async_computation.1 | async-start | bytes 4718592 | tf_op jit(solution)/shard_map/all_to_all | solution.py:125
  124.5 59.0 %all-to-all-start = ((bf16[8,144,2048]{2,1,0:T(8,128)(2,1)}), bf16[8,144,2048]{2,1,0:T(8,128)(2,1)}, u32[]{:S(2)}, u32[]{:S(2)}) async-start(bf16[8,144,2048]{2,1,0:T(8,128)(2,1)} %bitcast.236), calls=%async_computation | async-start | bytes 9437184 | tf_op jit(solution)/shard_map/all_to_all | solution.py:125
  198.5 32.9 %all-to-all-start.4 = ((bf16[8,144,1024]{2,1,0:T(8,128)(2,1)}), bf16[8,144,1024]{2,1,0:T(8,128)(2,1)S(1)}, u32[]{:S(2)}, u32[]{:S(2)}) async-start(bf16[8,144,1024]{2,1,0:T(8,128)(2,1)} %bitcast.245), calls=%async_computation.5 | async-start | bytes 4718592 | tf_op jit(solution)/shard_map/all_to_all | solution.py:125
  231.5 33.3 %all-to-all-start.3 = ((bf16[8,144,1024]{2,1,0:T(8,128)(2,1)}), bf16[8,144,1024]{2,1,0:T(8,128)(2,1)}, u32[]{:S(2)}, u32[]{:S(2)}) async-start(bf16[8,144,1024]{2,1,0:T(8,128)(2,1)} %bitcast.24), calls=%async_computation.3 | async-start | bytes 4718592 | tf_op jit(solution)/shard_map/all_to_all | solution.py:125
  235.9 59.5 %reduce-scatter.5.cloned.1.call-start = ((), (), s32[]{:S(2)}) async-start(), calls=%async_computation.10 | async-start | bytes 1310720 | tf_op jit(solution)/shard_map/reduce_scatter | solution.py:163
  238.5 56.9 %reduce-scatter.3.cloned.1.call-start = ((), (), s32[]{:S(2)}) async-start(), calls=%async_computation.9 | async-start | bytes 1310720 | tf_op jit(solution)/shard_map/reduce_scatter | solution.py:163
  244.4 20.4 %copy-start.25 = (f32[8,512]{1,0:T(8,128)S(1)}, f32[8,512]{1,0:T(8,128)}, u32[]{:S(2)}) copy-start(f32[8,512]{1,0:T(8,128)} %copy-done.24) | copy-start | bytes 49156
  244.9 24.1 %copy-start.26 = (f32[4,512]{1,0:T(4,128)}, f32[4,512]{1,0:T(4,128)S(1)}, u32[]{:S(2)}) copy-start(f32[4,512]{1,0:T(4,128)S(1)} %broadcast_maximum_fusion) | copy-start | bytes 24580
  297.0 1.2 collective-permute-start.5
  298.3 7.6 %collective-permute-start.8 = (f32[2048]{0:T(1024)S(1)}, f32[2048]{0:T(1024)S(1)}, u32[]{:S(2)}, u32[]{:S(2)}) collective-permute-start(f32[2048]{0:T(1024)S(1)} %bitcast.265), channel_id=1, source_target_pairs={{0,12},{4,0},{8,4},{12,8},{1,13},{5,1},{9,5},{13,9},{2,14},{6,2},{... | collective-permute-start | bytes 24584 | tf_op jit(solution)/shard_map/ppermute | solution.py:54
  299.4 6.5 %collective-permute-start.7 = (f32[2048]{0:T(1024)S(1)}, f32[2048]{0:T(1024)S(1)}, u32[]{:S(2)}, u32[]{:S(2)}) collective-permute-start(f32[2048]{0:T(1024)S(1)} %bitcast.266), channel_id=1, source_target_pairs={{0,8},{4,12},{8,0},{12,4},{1,9},{5,13},{9,1},{13,5},{2,10},{6,14},... | collective-permute-start | bytes 24584 | tf_op jit(solution)/shard_map/ppermute | solution.py:54
  300.8 5.1 %collective-permute-start.6 = (f32[2048]{0:T(1024)S(1)}, f32[2048]{0:T(1024)S(1)}, u32[]{:S(2)}, u32[]{:S(2)}) collective-permute-start(f32[2048]{0:T(1024)S(1)} %bitcast.267), channel_id=1, source_target_pairs={{0,4},{4,8},{8,12},{12,0},{1,5},{5,9},{9,13},{13,1},{2,6},{6,10},{... | collective-permute-start | bytes 24584 | tf_op jit(solution)/shard_map/ppermute | solution.py:54
  302.8 14.9 %collective-permute-start.2 = (bf16[128,2048]{1,0:T(8,128)(2,1)S(1)}, bf16[128,2048]{1,0:T(8,128)(2,1)S(1)}, u32[]{:S(2)}, u32[]{:S(2)}) collective-permute-start(bf16[128,2048]{1,0:T(8,128)(2,1)S(1)} %fusion.50), channel_id=1, source_target_pairs={{0,12},{4,0},{8,4},{12,8},{1,13},{5,1},{9,5},{13,9},{2,14},{6,2},{... | collective-permute-start | bytes 1572872 | tf_op jit(solution)/shard_map/ppermute | solution.py:54
  305.2 24.1 %collective-permute-start.1 = (bf16[128,2048]{1,0:T(8,128)(2,1)S(1)}, bf16[128,2048]{1,0:T(8,128)(2,1)S(1)}, u32[]{:S(2)}, u32[]{:S(2)}) collective-permute-start(bf16[128,2048]{1,0:T(8,128)(2,1)S(1)} %fusion.50), channel_id=1, source_target_pairs={{0,8},{4,12},{8,0},{12,4},{1,9},{5,13},{9,1},{13,5},{2,10},{6,14},... | collective-permute-start | bytes 1572872 | tf_op jit(solution)/shard_map/ppermute | solution.py:54
  305.8 23.5 %collective-permute-start = (bf16[128,2048]{1,0:T(8,128)(2,1)S(1)}, bf16[128,2048]{1,0:T(8,128)(2,1)S(1)}, u32[]{:S(2)}, u32[]{:S(2)}) collective-permute-start(bf16[128,2048]{1,0:T(8,128)(2,1)S(1)} %fusion.50), channel_id=1, source_target_pairs={{0,4},{4,8},{8,12},{12,0},{1,5},{5,9},{9,13},{13,1},{2,6},{6,10},{... | collective-permute-start | bytes 1572872 | tf_op jit(solution)/shard_map/ppermute | solution.py:54
  306.0 3.7 collective-permute-start.11
  308.4 4.5 %collective-permute-start.10 = (f32[2048]{0:T(1024)S(1)}, f32[2048]{0:T(1024)S(1)}, u32[]{:S(2)}, u32[]{:S(2)}) collective-permute-start(f32[2048]{0:T(1024)S(1)} %bitcast.269), channel_id=1, source_target_pairs={{0,2},{1,3},{2,0},{3,1},{4,6},{5,7},{6,4},{7,5},{8,10},{9,11},{10,... | collective-permute-start | bytes 24584 | tf_op jit(solution)/shard_map/ppermute | solution.py:54
  309.7 5.4 %collective-permute-start.9 = (f32[2048]{0:T(1024)S(1)}, f32[2048]{0:T(1024)S(1)}, u32[]{:S(2)}, u32[]{:S(2)}) collective-permute-start(f32[2048]{0:T(1024)S(1)} %bitcast.270), channel_id=1, source_target_pairs={{0,1},{1,2},{2,3},{3,0},{4,5},{5,6},{6,7},{7,4},{8,9},{9,10},{10,1... | collective-permute-start | bytes 24584 | tf_op jit(solution)/shard_map/ppermute | solution.py:54
  341.4 7.8 %collective-permute-start.12 = (bf16[256,2048]{1,0:T(8,128)(2,1)}, bf16[256,2048]{1,0:T(8,128)(2,1)}, u32[]{:S(2)}, u32[]{:S(2)}) collective-permute-start(bf16[256,2048]{1,0:T(8,128)(2,1)} %fusion.66), channel_id=1, source_target_pairs={{0,16},{16,0},{1,17},{17,1},{2,18},{18,2},{3,19},{19,3},{4,20},{20... | collective-permute-start | bytes 3145736 | tf_op jit(solution)/shard_map/ppermute | solution.py:43
  348.1 6.9 %collective-permute-start.4 = (bf16[4,128,128]{2,1,0:T(8,128)(2,1)S(1)}, bf16[4,128,128]{2,1,0:T(8,128)(2,1)S(1)}, u32[]{:S(2)}, u32[]{:S(2)}) collective-permute-start(bf16[4,128,128]{2,1,0:T(8,128)(2,1)S(1)} %fusion.98), channel_id=1, source_target_pairs={{0,16},{16,0},{1,17},{17,1},{2,18},{18,2},{3,19},{19,3},{4,20},{20... | collective-permute-start | bytes 393224 | tf_op jit(solution)/shard_map/ppermute | solution.py:43
  348.8 6.9 %collective-permute-start.3 = (bf16[4,128,128]{2,1,0:T(8,128)(2,1)S(1)}, bf16[4,128,128]{2,1,0:T(8,128)(2,1)S(1)}, u32[]{:S(2)}, u32[]{:S(2)}) collective-permute-start(bf16[4,128,128]{2,1,0:T(8,128)(2,1)S(1)} %fusion.97), channel_id=1, source_target_pairs={{0,16},{16,0},{1,17},{17,1},{2,18},{18,2},{3,19},{19,3},{4,20},{20... | collective-permute-start | bytes 393224 | tf_op jit(solution)/shard_map/ppermute | solution.py:43
  349.2 28.7 %copy-start.1 = (bf16[1,768,2048]{2,1,0:T(8,128)(2,1)S(1)}, bf16[1,768,2048]{2,1,0:T(8,128)(2,1)}, u32[]{:S(2)}) copy-start(bf16[1,768,2048]{2,1,0:T(8,128)(2,1)} %param.23) | copy-start | bytes 9437188
  351.1 11.1 %collective-permute-start.13 = (bf16[64,2048]{1,0:T(8,128)(2,1)S(1)}, bf16[64,2048]{1,0:T(8,128)(2,1)S(1)}, u32[]{:S(2)}, u32[]{:S(2)}) collective-permute-start(bf16[64,2048]{1,0:T(8,128)(2,1)S(1)} %get-tuple-element.25), channel_id=1, source_target_pairs={{0,1},{1,2},{2,3},{3,0},{4,5},{5,6},{6,7},{7,4},{8,9},{9,10},{10,1... | collective-permute-start | bytes 786440 | tf_op jit(solution)/shard_map/ppermute | solution.py:43
  351.1 14.4 %collective-permute-start.15 = (bf16[64,2048]{1,0:T(8,128)(2,1)S(1)}, bf16[64,2048]{1,0:T(8,128)(2,1)S(1)}, u32[]{:S(2)}, u32[]{:S(2)}) collective-permute-start(bf16[64,2048]{1,0:T(8,128)(2,1)S(1)} %get-tuple-element.26), channel_id=1, source_target_pairs={{0,3},{1,0},{2,1},{3,2},{4,7},{5,4},{6,5},{7,6},{8,11},{9,8},{10,9... | collective-permute-start | bytes 786440 | tf_op jit(solution)/shard_map/ppermute | solution.py:43
  355.0 22.2 %collective-permute-start.14 = (bf16[64,2048]{1,0:T(8,128)(2,1)S(1)}, bf16[64,2048]{1,0:T(8,128)(2,1)S(1)}, u32[]{:S(2)}, u32[]{:S(2)}) collective-permute-start(bf16[64,2048]{1,0:T(8,128)(2,1)S(1)} %get-tuple-element.27), channel_id=1, source_target_pairs={{0,2},{1,3},{2,0},{3,1},{4,6},{5,7},{6,4},{7,5},{8,10},{9,11},{10,... | collective-permute-start | bytes 786440 | tf_op jit(solution)/shard_map/ppermute | solution.py:43
  (37 other events, 168.2 us)
Sparse Core Ops, SparseCore 0:
  10.2 30.8 all-gather.6
  43.2 27.5 all-gather.4
  72.4 45.4 all-gather.8
  238.7 26.2 reduce-scatter.4
  269.2 24.5 reduce-scatter.2
